TPU v7x, 512 devices: a whole 4x4x16 slice. The times are simulated.
512 devices in a mesh: dp: 16 (over x, y), fsdp: 32 (over z, core).
Axes of the slice: x: 4, y: 4, z: 16, core: 2. Of those that a mesh axis runs over, the one named last changes fastest.
Arguments:
- owners: int32 [576], P('dp'), parts along dimension 0, may hold values from 0 to 31, as said below
- grads: bfloat16 [64, 512, 4608], P('dp', 'fsdp'), parts along dimension 0, may hold values from -1.1953125 to 1.1953125
- roots: bfloat16 [1024, 2, 512, 512], P(('dp', 'fsdp')), parts along dimension 0, may hold values from -1 to 3, as said below
Outputs:
- direction: bfloat16 [64, 512, 4608], P('dp', 'fsdp'), parts along dimension 0
- grams: bfloat16 [1024, 2, 512, 512], P(('dp', 'fsdp')), parts along dimension 0
There are 16 independent parts, one for each index of `dp`. A program takes and returns all parts, laid end to end along the dimension named above; each array names one. Nothing has to cross between parts.
Inputs may be any that keep to these rules, and one draw needn't show every extreme that they name: `owners`: no device is assigned more than 2 blocks, and some device exactly 2. `roots`: each factor is symmetric.
All inputs are finite; a program needn't handle non-finite values.
Results may differ from a plain program's by a relative error of at most 0.0049.
Values may be sent and summed in bfloat16 or wider, within the bound.
A program may use at most 128 MiB of HBM per device.

v0:
```python
import jax
import jax.numpy as jnp
from jax import lax
from jax.sharding import PartitionSpec as P


def send_back(direction_blocks, slot_count, devices_here, row_count, block_order):
    shaped = direction_blocks.reshape(slot_count, devices_here, row_count, block_order)
    return lax.all_to_all(shaped, "fsdp", split_axis=1, concat_axis=1, tiled=True)


def gram_pair(blocks):
    gram_left = jnp.einsum("mac,mbc->mab", blocks, blocks, preferred_element_type=jnp.float32)
    gram_right = jnp.einsum("mca,mcb->mab", blocks, blocks, preferred_element_type=jnp.float32)
    return jnp.stack([gram_left.astype(jnp.bfloat16), gram_right.astype(jnp.bfloat16)], axis=1)


def local(owners, grads, roots):
    devices_here = lax.axis_size("fsdp")
    slab_count, row_count, columns = grads.shape
    slot_count = roots.shape[0]
    block_order = roots.shape[-1]
    column_blocks = columns // block_order
    block_total = slab_count * column_blocks
    position = jnp.arange(block_total, dtype=jnp.int32)
    same_owner = owners[:, None] == owners[None, :]
    order_within = jnp.sum(same_owner & (position[None, :] < position[:, None]), axis=1)
    slot_code = owners * slot_count + order_within
    targets = jnp.arange(devices_here * slot_count, dtype=jnp.int32)
    placing = (slot_code[:, None] == targets[None, :]).astype(jnp.bfloat16)
    placing = placing.reshape(slab_count, column_blocks, devices_here, slot_count)
    grads_four = grads.reshape(slab_count, row_count, column_blocks, block_order)
    outgoing = jnp.einsum(
        "sjdm,srjc->mdrc", placing, grads_four, preferred_element_type=jnp.float32
    ).astype(jnp.bfloat16)
    arrived = lax.all_to_all(outgoing, "fsdp", split_axis=1, concat_axis=1, tiled=True)
    blocks = arrived.reshape(slot_count, devices_here * row_count, block_order)
    product = jnp.einsum(
        "mac,mcb->mab", blocks, roots[:, 1], preferred_element_type=jnp.float32
    ).astype(jnp.bfloat16)
    direction_blocks = jnp.einsum(
        "mac,mcb->mab", roots[:, 0], product, preferred_element_type=jnp.float32
    ).astype(jnp.bfloat16)
    gram_pairs = gram_pair(blocks)
    returned = send_back(direction_blocks, slot_count, devices_here, row_count, block_order)
    result = jnp.einsum(
        "sjdm,mdrc->srjc", placing, returned, preferred_element_type=jnp.float32
    ).astype(jnp.bfloat16)
    return (result.reshape(slab_count, row_count, columns), gram_pairs)


def solution(mesh):
    return jax.shard_map(
        local,
        mesh=mesh,
        in_specs=(P("dp"), P("dp", "fsdp", None), P(("dp", "fsdp"), None, None, None)),
        out_specs=(P("dp", "fsdp", None), P(("dp", "fsdp"), None, None, None)),
        check_vma=False,
    )
```

profile of v0, /device:TPU:1, one launch (start us, length us, event | category | flops | bytes accessed | tf_op | source)
XLA Modules:
  0.0 144.2 jit_solution(7700178965578282854)
XLA Ops:
  0.6 1.4 reshape.34
  2.0 0.9 convert_reduce_fusion
  3.0 0.7 multiply_add_fusion.1
  3.6 0.1 eq.38
  3.7 0.6 fusion.2
  4.3 0.6 copy.33
  4.8 72.3 %all_to_all.10 = bf16[2,32,16,512]{3,2,0,1:T(8,128)(2,1)S(1)} all-to-all(bf16[2,32,16,512]{3,2,0,1:T(8,128)(2,1)S(1)} %copy.33), channel_id=1, replica_groups=mesh['dp'=16,'fsdp'=32] {'fsdp'}, dimensions={1} | all-to-all | bytes 2097152 | tf_op jit(solution)/shard_map/all_to_all | solution.py:36
  77.1 0.1 copy.34
  77.2 2.8 %convolution_convert_fusion = bf16[2,512,512]{1,2,0:T(8,128)(2,1)S(1)} fusion(bf16[2,512,512]{2,1,0:T(8,128)(2,1)S(1)} %bitcast.50, bf16[2,2,512,512]{3,2,1,0:T(8,128)(2,1)} %param.5), kind=kOutput, calls=%fused_computation.3 | convolution fusion | flops 1074790400 | bytes 4194304 | tf_op jit(solution)/shard_map/mac,mcb->mab/dot_general | solution.py:41
  80.0 2.1 %copy.37 = bf16[2,32,16,512]{3,0,2,1:T(2,128)(2,1)} copy(bf16[2,32,16,512]{3,2,1,0:T(8,128)(2,1)S(1)} %bitcast.54) | data formatting | bytes 2097152 | tf_op jit(solution)/shard_map/reshape | solution.py:8
  82.1 4.1 %all-to-all-start.1 = ((bf16[2,32,16,512]{3,0,2,1:T(2,128)(2,1)}), bf16[2,32,16,512]{3,0,2,1:T(2,128)(2,1)S(1)}, u32[]{:S(2)}, u32[]{:S(2)}) async-start(bf16[2,32,16,512]{3,0,2,1:T(2,128)(2,1)} %copy.37), calls=%async_computation.1 | async-start | bytes 2097152 | tf_op jit(solution)/shard_map/all_to_all | solution.py:9
  86.2 0.8 fusion.1
  86.9 0.7 fusion
  87.7 0.2 pad_maximum_fusion
  87.9 1.5 %copy.41 = bf16[2,2,512,512]{3,2,1,0:T(8,128)(2,1)} copy(bf16[2,2,512,512]{3,2,0,1:T(8,128)(2,1)S(1)} %pad_maximum_fusion) | data formatting | bytes 4194304
  89.3 52.7 %all-to-all-done.1 = bf16[2,32,16,512]{3,0,2,1:T(2,128)(2,1)S(1)} async-done(((bf16[2,32,16,512]{3,0,2,1:T(2,128)(2,1)}), bf16[2,32,16,512]{3,0,2,1:T(2,128)(2,1)S(1)}, u32[]{:S(2)}, u32[]{:S(2)}) %all-to-all-start.1) | async-done | bytes 1048608 | tf_op jit(solution)/shard_map/all_to_all | solution.py:9
  142.0 0.9 fusion.3
  142.9 0.4 reshape.44
  143.3 0.9 copy.51
  (1 shorter events, 0.0 us)
Async XLA Ops:
  82.1 59.9 %all-to-all-start.1 = ((bf16[2,32,16,512]{3,0,2,1:T(2,128)(2,1)}), bf16[2,32,16,512]{3,0,2,1:T(2,128)(2,1)S(1)}, u32[]{:S(2)}, u32[]{:S(2)}) async-start(bf16[2,32,16,512]{3,0,2,1:T(2,128)(2,1)} %copy.37), calls=%async_computation.1 | async-start | bytes 2097152 | tf_op jit(solution)/shard_map/all_to_all | solution.py:9
where the time goes:
time: 145 us; the launch traced here: 144 us
  blocking collectives  72.3 us (50%)
  waiting for transfers between devices  52.7 us (36%)
  local copies, waits for them, and re-layouts  6.95 us (5%)
  matrix products  5.78 us (4%)
  starting transfers between devices  4.08 us (3%)
  other arithmetic  1.78 us (1%)
    all_to_all x1, blocking collectives, local(): lax.all_to_all(outgoing, 'fsdp', split_axis=1, concat_axis=1, tiled=True)  72.3 us
    all_to_all x1, waiting for transfers between devices, send_back(): lax.all_to_all(shaped, 'fsdp', split_axis=1, concat_axis=1, tiled=True)  52.7 us
    all_to_all x1, starting transfers between devices, send_back(): lax.all_to_all(shaped, 'fsdp', split_axis=1, concat_axis=1, tiled=True)  4.08 us
  transfers between devices with their start and end apart: 1, of which 1 were waited for; matrix products, arithmetic and copies ran while one was open for 2% of the time, Pallas kernels for 0%

commit v1 on v0

v1 whole, which is shorter than its diff:
```python
import functools

import jax
import jax.numpy as jnp
from jax import lax
from jax.experimental import pallas as pl
from jax.experimental.pallas import tpu as pltpu
from jax.sharding import PartitionSpec as P

MESH = pl.DeviceIdType.MESH


def offsets(chips):
    order = [(0, 1)]
    for distance in range(1, chips // 2 + 1):
        for step in sorted({distance, chips - distance}):
            order += [(step, 0), (step, 1)]
    return order


def kernel(
    sizes, owners_ref, grads_ref, roots_ref, dir_ref, grams_ref,
    gv, packed, blocks, roots_v, outgoing, returned, dir_v, grams_v, table_v, table,
    load_sem, table_sem, roots_sem, send_sem, recv_sem, out_sem,
):
    devices, slabs, ncol, rows, order, slots = sizes
    total = slabs * ncol
    chips = devices // 2
    me = lax.axis_index("fsdp")
    z, core = me // 2, lax.rem(me, 2)
    partners = offsets(chips)

    def device(step, other):
        return lax.rem(z + step, chips) * 2 + lax.rem(core + other, 2)

    barrier = pltpu.get_barrier_semaphore()
    for step, other in partners:
        pl.semaphore_signal(
            barrier, inc=1, device_id={"fsdp": device(step, other)}, device_id_type=MESH
        )

    loads = []
    for k in range(total):
        s, j = divmod(k, ncol)
        loads.append(
            pltpu.make_async_copy(
                grads_ref.at[s, :, pl.ds(j * order, order)], gv.at[k], load_sem.at[k]
            )
        )
    for copy in loads:
        copy.start()
    roots_copy = pltpu.make_async_copy(roots_ref, roots_v, roots_sem)
    roots_copy.start()

    lane = lax.broadcasted_iota(jnp.int32, (8, 128), 1)
    first = jnp.full((8, 128), -1, jnp.int32)
    last = jnp.full((8, 128), -1, jnp.int32)
    for k in range(total):
        last = jnp.where(lane == owners_ref[k], k, last)
        first = jnp.where(lane == owners_ref[total - 1 - k], total - 1 - k, first)
    table_v[0] = first
    table_v[1] = jnp.where(first == last, -1, last)
    table_copy = pltpu.make_async_copy(table_v, table, table_sem)
    table_copy.start()
    table_copy.wait()
    for copy in loads:
        copy.wait()

    def pack(d, carry):
        for m in range(slots):
            packed[m, d] = gv[jnp.maximum(table[m, 0, d], 0)]
        return carry

    lax.fori_loop(0, devices, pack, 0)
    pl.semaphore_wait(barrier, len(partners))

    mine = pl.ds(pl.multiple_of(me * rows, rows), rows)
    for m in range(slots):
        pltpu.make_async_copy(
            packed.at[m, me], blocks.at[m, mine, :], recv_sem.at[0, m]
        ).start()
        for step, other in partners:
            to = device(step, other)
            pltpu.make_async_remote_copy(
                src_ref=packed.at[m, to],
                dst_ref=blocks.at[m, mine, :],
                send_sem=send_sem.at[0, m],
                recv_sem=recv_sem.at[0, m],
                device_id={"fsdp": to},
                device_id_type=MESH,
            ).start()

    roots_copy.wait()
    for m in range(slots):
        pltpu.make_async_copy(blocks.at[m], blocks.at[m], recv_sem.at[0, m]).wait()
        block = blocks[m]
        product = jnp.dot(
            block, roots_v[m, 1], preferred_element_type=jnp.float32
        ).astype(jnp.bfloat16)
        outgoing[m] = jnp.dot(
            roots_v[m, 0], product, preferred_element_type=jnp.float32
        ).astype(jnp.bfloat16)
        pltpu.make_async_copy(
            outgoing.at[m, mine, :], returned.at[m, me], recv_sem.at[1, m]
        ).start()
        for step, other in partners:
            to = device(step, other)
            pltpu.make_async_remote_copy(
                src_ref=outgoing.at[m, pl.ds(pl.multiple_of(to * rows, rows), rows), :],
                dst_ref=returned.at[m, me],
                send_sem=send_sem.at[1, m],
                recv_sem=recv_sem.at[1, m],
                device_id={"fsdp": to},
                device_id_type=MESH,
            ).start()
        kept = jnp.where(table[m, 0, me] >= 0, block, jnp.zeros_like(block))
        grams_v[m, 0] = lax.dot_general(
            kept, kept, (((1,), (1,)), ((), ())), preferred_element_type=jnp.float32
        ).astype(jnp.bfloat16)
        grams_v[m, 1] = lax.dot_general(
            kept, kept, (((0,), (0,)), ((), ())), preferred_element_type=jnp.float32
        ).astype(jnp.bfloat16)
        pltpu.make_async_copy(grams_v.at[m], grams_ref.at[m], out_sem.at[m]).start()

    for m in range(slots):
        pltpu.make_async_copy(
            returned.at[m], returned.at[m], recv_sem.at[1, m]
        ).wait()
    for k in range(total):
        s, j = divmod(k, ncol)
        owner = owners_ref[k]
        slot = jnp.where(table[0, 0, owner] == k, 0, 1)
        dir_v[s, :, j * order : (j + 1) * order] = returned[slot, owner]
    dir_copy = pltpu.make_async_copy(dir_v, dir_ref, out_sem.at[slots])
    dir_copy.start()
    dir_copy.wait()
    others = pl.ds(0, devices - 1)
    for m in range(slots):
        pltpu.make_async_copy(grams_v.at[m], grams_ref.at[m], out_sem.at[m]).wait()
        for phase in range(2):
            pltpu.make_async_copy(
                packed.at[m, others], packed.at[m, others], send_sem.at[phase, m]
            ).wait()


def local(owners, grads, roots):
    devices = lax.axis_size("fsdp")
    slabs, rows, columns = grads.shape
    slots, _, order, _ = roots.shape
    ncol = columns // order
    sizes = (devices, slabs, ncol, rows, order, slots)
    any_spec = pl.BlockSpec(memory_space=pl.ANY)
    bf16 = jnp.bfloat16
    return pl.pallas_call(
        functools.partial(kernel, sizes),
        out_shape=(
            jax.ShapeDtypeStruct(grads.shape, bf16),
            jax.ShapeDtypeStruct(roots.shape, bf16),
        ),
        in_specs=[pl.BlockSpec(memory_space=pltpu.SMEM), any_spec, any_spec],
        out_specs=(any_spec, any_spec),
        scratch_shapes=[
            pltpu.VMEM((slabs * ncol, rows, order), bf16),
            pltpu.VMEM((slots, devices, rows, order), bf16),
            pltpu.VMEM((slots, order, order), bf16),
            pltpu.VMEM(roots.shape, bf16),
            pltpu.VMEM((slots, order, order), bf16),
            pltpu.VMEM((slots, devices, rows, order), bf16),
            pltpu.VMEM(grads.shape, bf16),
            pltpu.VMEM(roots.shape, bf16),
            pltpu.VMEM((2, 8, 128), jnp.int32),
            pltpu.SMEM((2, 8, 128), jnp.int32),
            pltpu.SemaphoreType.DMA((slabs * ncol,)),
            pltpu.SemaphoreType.DMA,
            pltpu.SemaphoreType.DMA,
            pltpu.SemaphoreType.DMA((2, slots)),
            pltpu.SemaphoreType.DMA((2, slots)),
            pltpu.SemaphoreType.DMA((slots + 1,)),
        ],
        compiler_params=pltpu.CompilerParams(
            collective_id=0, has_side_effects=True, vmem_limit_bytes=32 << 20
        ),
        cost_estimate=pl.CostEstimate(
            flops=slots * 4 * 2 * order**3, bytes_accessed=6 << 20, transcendentals=0
        ),
    )(owners, grads, roots)


def solution(mesh):
    return jax.shard_map(
        local,
        mesh=mesh,
        in_specs=(P("dp"), P("dp", "fsdp", None), P(("dp", "fsdp"), None, None, None)),
        out_specs=(P("dp", "fsdp", None), P(("dp", "fsdp"), None, None, None)),
        check_vma=False,
    )
```

time: 145 us -> 116 us (0.80); the launches traced: 144 us -> 114 us
  Pallas kernels: 0 us -> 108 us
  blocking collectives: 72.3 us -> 0 us
  waiting for transfers between devices: 52.7 us -> 0 us
  matrix products: 5.78 us -> 0 us
  starting transfers between devices: 4.08 us -> 0 us
  other arithmetic: 1.78 us -> 0 us
  local copies, waits for them, and re-layouts: 6.95 us -> 5.44 us
    pallas_call x0 -> x1, Pallas kernels: none -> 108 us  [local(): pl.pallas_call(functools.partial(kernel, sizes), out_shape=(jax.ShapeDtyp...]
    all_to_all x1 -> x0, blocking collectives: 72.3 us -> none  [local(): lax.all_to_all(outgoing, 'fsdp', split_axis=1, concat_axis=1, tiled=True)]
    all_to_all x1 -> x0, waiting for transfers between devices: 52.7 us -> none  [send_back(): lax.all_to_all(shaped, 'fsdp', split_axis=1, concat_axis=1, tiled=True)]
    dot_general x5 -> x0, matrix products: 5.78 us -> none  [the longest x1 2.8 us: local(): jnp.einsum('mac,mcb->mab', roots[:, 0], product, preferred_element_type=j...]
    reshape x4 -> x0, local copies, waits for them, and re-layouts: 4.76 us -> none  [the longest x1 2.07 us: send_back(): direction_blocks.reshape(slot_count, devices_here, row_count, block_order)]
    all_to_all x1 -> x0, starting transfers between devices: 4.08 us -> none  [send_back(): lax.all_to_all(shaped, 'fsdp', split_axis=1, concat_axis=1, tiled=True)]
    unnamed x1 -> x8, local copies, waits for them, and re-layouts: 1.45 us -> 5.44 us
  transfers between devices with their start and end apart: 1 -> 0, of which waited for: 1 -> 0; matrix products, arithmetic and copies ran while one was open for 2% -> 0% of each run, Pallas kernels for 0% -> 0%
where the time goes in v1:
time: 116 us; the launch traced here: 114 us
  Pallas kernels  108 us (93%)
  local copies, waits for them, and re-layouts  5.44 us (5%)
    pallas_call x1, Pallas kernels, local(): pl.pallas_call(functools.partial(kernel, sizes), out_shape=(jax.ShapeDtyp...  108 us
    unnamed x8, local copies, waits for them, and re-layouts  5.44 us

profile of v1, /device:TPU:1, one launch (start us, length us, event | category | flops | bytes accessed | tf_op | source)
XLA Modules:
  0.0 113.6 jit_solution(16466939715814808014)
XLA Ops:
  0.6 0.0 copy-start
  0.6 1.6 %copy-done = bf16[2,2,512,512]{3,2,1,0:T(8,128)(2,1)S(1)} copy-done((bf16[2,2,512,512]{3,2,1,0:T(8,128)(2,1)S(1)}, bf16[2,2,512,512]{3,2,1,0:T(8,128)(2,1)}, u32[]{:S(2)}) %copy-start) | copy-done | bytes 2097176
  2.2 0.0 copy-start.1
  2.2 1.1 copy-done.1
  3.3 0.0 copy-start.2
  3.3 0.7 copy-done.2
  3.9 107.6 %shard_map.50 = (bf16[4,16,4608]{2,1,0:T(8,128)(2,1)S(1)}, bf16[2,2,512,512]{3,2,1,0:T(8,128)(2,1)S(1)}) custom-call(s32[36]{0:T(128)S(1)} %copy-done.2, bf16[4,16,4608]{2,1,0:T(8,128)(2,1)S(1)} %copy-done.1, bf16[2,2,512,512]{3,2,1,0:T(8,128)(2,1)S(1)} %copy-done), custom_call_target="tpu_custom_call" | custom-call | flops 2147483648 | bytes 6291456 | tf_op jit(solution)/shard_map/pallas_call | solution.py:154
  111.5 0.8 copy.7
  112.3 1.3 %copy.8 = bf16[2,2,512,512]{3,2,1,0:T(8,128)(2,1)} copy(bf16[2,2,512,512]{3,2,1,0:T(8,128)(2,1)S(1)} %get-tuple-element.5) | data formatting | bytes 4194304
Async XLA Ops:
  0.6 1.6 %copy-start = (bf16[2,2,512,512]{3,2,1,0:T(8,128)(2,1)S(1)}, bf16[2,2,512,512]{3,2,1,0:T(8,128)(2,1)}, u32[]{:S(2)}) copy-start(bf16[2,2,512,512]{3,2,1,0:T(8,128)(2,1)} %roots_ref.1) | copy-start | bytes 6291460
  2.2 1.1 copy-start.1
  3.3 0.7 copy-start.2

commit v2 on v1

v2 whole, which is shorter than its diff:
```python
import functools

import jax
import jax.numpy as jnp
from jax import lax
from jax.experimental import pallas as pl
from jax.experimental.pallas import tpu as pltpu
from jax.sharding import PartitionSpec as P

MESH = pl.DeviceIdType.MESH


def rings(chips):
    groups, near, far = [], 0, 1
    while near < chips // 2:
        group = [(0, 1)] if near == 0 else []
        for distance in range(near + 1, min(far, chips // 2) + 1):
            for step in sorted({distance, chips - distance}):
                group += [(step, 0), (step, 1)]
        groups.append(group)
        near, far = far, 2 * far
    return groups


def exchange(
    sizes, owners_ref, grads_ref, roots_ref, dir_v, grams_v,
    gv, packed, blocks, roots_v, outgoing, returned, table_v, table, owners,
    load_sem, table_sem, roots_sem, near_sem, send_sem, recv_sem,
):
    devices, slabs, ncol, rows, order, slots = sizes
    total = slabs * ncol
    chips = devices // 2
    me = lax.axis_index("fsdp")
    z, core = me // 2, lax.rem(me, 2)
    groups = rings(chips)

    def device(step, other):
        return lax.rem(z + step, chips) * 2 + lax.rem(core + other, 2)

    def signal(semaphore, to):
        pl.semaphore_signal(
            semaphore, inc=1, device_id={"fsdp": to}, device_id_type=MESH
        )

    barrier = pltpu.get_barrier_semaphore()
    for step, other in groups[0]:
        signal(barrier, device(step, other))

    owners_copy = pltpu.make_async_copy(owners_ref, owners, table_sem)
    owners_copy.start()
    loads = []
    for k in range(total):
        s, j = divmod(k, ncol)
        loads.append(
            pltpu.make_async_copy(
                grads_ref.at[s, :, pl.ds(j * order, order)], gv.at[k], load_sem.at[k]
            )
        )
    for copy in loads:
        copy.start()
    roots_copy = pltpu.make_async_copy(roots_ref, roots_v, roots_sem)
    roots_copy.start()

    owners_copy.wait()
    lane = lax.broadcasted_iota(jnp.int32, (8, 128), 1)
    first = jnp.full((8, 128), -1, jnp.int32)
    last = jnp.full((8, 128), -1, jnp.int32)
    for k in range(total):
        last = jnp.where(lane == owners[k], k, last)
        first = jnp.where(lane == owners[total - 1 - k], total - 1 - k, first)
    table_v[0] = first
    table_v[1] = jnp.where(first == last, -1, last)
    table_copy = pltpu.make_async_copy(table_v, table, table_sem)
    table_copy.start()
    table_copy.wait()
    for copy in loads:
        copy.wait()

    mine = pl.ds(pl.multiple_of(me * rows, rows), rows)

    def pack(m, d):
        packed[m, d] = gv[jnp.maximum(table[m, 0, d], 0)]

    for m in range(slots):
        pack(m, me)
        pltpu.make_async_copy(
            packed.at[m, me], blocks.at[m, mine, :], recv_sem.at[0, m]
        ).start()

    for stage, group in enumerate(groups):
        if stage == 0:
            pl.semaphore_wait(barrier, len(group))
        else:
            reach = 2 ** (stage - 1)
            signal(near_sem.at[stage - 1], device(reach, 0))
            signal(near_sem.at[stage - 1], device(chips - reach, 0))
            pl.semaphore_wait(near_sem.at[stage - 1], 2)
        for m in range(slots):
            for step, other in group:
                to = device(step, other)
                pack(m, to)
                pltpu.make_async_remote_copy(
                    src_ref=packed.at[m, to],
                    dst_ref=blocks.at[m, mine, :],
                    send_sem=send_sem.at[0, m],
                    recv_sem=recv_sem.at[0, m],
                    device_id={"fsdp": to},
                    device_id_type=MESH,
                ).start()

    roots_copy.wait()
    backward = [partner for group in groups for partner in group][::-1]
    for m in range(slots):
        pltpu.make_async_copy(blocks.at[m], blocks.at[m], recv_sem.at[0, m]).wait()
        block = blocks[m]
        product = jnp.dot(
            block, roots_v[m, 1], preferred_element_type=jnp.float32
        ).astype(jnp.bfloat16)
        outgoing[m] = jnp.dot(
            roots_v[m, 0], product, preferred_element_type=jnp.float32
        ).astype(jnp.bfloat16)
        for step, other in backward:
            to = device(step, other)
            pltpu.make_async_remote_copy(
                src_ref=outgoing.at[m, pl.ds(pl.multiple_of(to * rows, rows), rows), :],
                dst_ref=returned.at[m, me],
                send_sem=send_sem.at[1, m],
                recv_sem=recv_sem.at[1, m],
                device_id={"fsdp": to},
                device_id_type=MESH,
            ).start()
        pltpu.make_async_copy(
            outgoing.at[m, mine, :], returned.at[m, me], recv_sem.at[1, m]
        ).start()
        kept = jnp.where(table[m, 0, me] >= 0, block, jnp.zeros_like(block))
        grams_v[m, 0] = lax.dot_general(
            kept, kept, (((1,), (1,)), ((), ())), preferred_element_type=jnp.float32
        ).astype(jnp.bfloat16)
        grams_v[m, 1] = lax.dot_general(
            kept, kept, (((0,), (0,)), ((), ())), preferred_element_type=jnp.float32
        ).astype(jnp.bfloat16)

    others = pl.ds(0, devices - 1)
    for m in range(slots):
        pltpu.make_async_copy(
            packed.at[m, others], packed.at[m, others], send_sem.at[0, m]
        ).wait()
    for m in range(slots):
        pltpu.make_async_copy(
            packed.at[m, others], packed.at[m, others], send_sem.at[1, m]
        ).wait()
        pltpu.make_async_copy(
            returned.at[m], returned.at[m], recv_sem.at[1, m]
        ).wait()
    for k in range(total):
        s, j = divmod(k, ncol)
        owner = owners[k]
        slot = jnp.where(table[0, 0, owner] == k, 0, 1)
        dir_v[s, :, j * order : (j + 1) * order] = returned[slot, owner]


def store(dir_in, grams_in, dir_ref, grams_ref, sems):
    copies = [
        pltpu.make_async_copy(grams_in, grams_ref, sems.at[0]),
        pltpu.make_async_copy(dir_in, dir_ref, sems.at[1]),
    ]
    for copy in copies:
        copy.start()
    for copy in copies:
        copy.wait()


def local(owners, grads, roots):
    devices = lax.axis_size("fsdp")
    slabs, rows, columns = grads.shape
    slots, _, order, _ = roots.shape
    ncol = columns // order
    total = slabs * ncol
    sizes = (devices, slabs, ncol, rows, order, slots)
    hbm = pl.BlockSpec(memory_space=pltpu.HBM)
    vmem = pl.BlockSpec(memory_space=pltpu.VMEM)
    bf16 = jnp.bfloat16
    stages = len(rings(devices // 2))
    owners, grads, roots = (
        pltpu.with_memory_space_constraint(x, pltpu.HBM) for x in (owners, grads, roots)
    )
    direction, grams = pl.pallas_call(
        functools.partial(exchange, sizes),
        out_shape=(pltpu.VMEM(grads.shape, bf16), pltpu.VMEM(roots.shape, bf16)),
        in_specs=[hbm, hbm, hbm],
        out_specs=(vmem, vmem),
        scratch_shapes=[
            pltpu.VMEM((total, rows, order), bf16),
            pltpu.VMEM((slots, devices, rows, order), bf16),
            pltpu.VMEM((slots, order, order), bf16),
            pltpu.VMEM(roots.shape, bf16),
            pltpu.VMEM((slots, order, order), bf16),
            pltpu.VMEM((slots, devices, rows, order), bf16),
            pltpu.VMEM((2, 8, 128), jnp.int32),
            pltpu.SMEM((2, 8, 128), jnp.int32),
            pltpu.SMEM((total,), jnp.int32),
            pltpu.SemaphoreType.DMA((total,)),
            pltpu.SemaphoreType.DMA,
            pltpu.SemaphoreType.DMA,
            pltpu.SemaphoreType.REGULAR((stages - 1,)),
            pltpu.SemaphoreType.DMA((2, slots)),
            pltpu.SemaphoreType.DMA((2, slots)),
        ],
        compiler_params=pltpu.CompilerParams(
            collective_id=0, has_side_effects=True, vmem_limit_bytes=32 << 20
        ),
        cost_estimate=pl.CostEstimate(
            flops=slots * 4 * 2 * order**3, bytes_accessed=6 << 20, transcendentals=0
        ),
    )(owners, grads, roots)
    return pl.pallas_call(
        store,
        out_shape=(
            jax.ShapeDtypeStruct(grads.shape, bf16),
            jax.ShapeDtypeStruct(roots.shape, bf16),
        ),
        in_specs=[vmem, vmem],
        out_specs=(hbm, hbm),
        scratch_shapes=[pltpu.SemaphoreType.DMA((2,))],
        compiler_params=pltpu.CompilerParams(vmem_limit_bytes=16 << 20),
    )(direction, grams)


def solution(mesh):
    return jax.shard_map(
        local,
        mesh=mesh,
        in_specs=(P("dp"), P("dp", "fsdp", None), P(("dp", "fsdp"), None, None, None)),
        out_specs=(P("dp", "fsdp", None), P(("dp", "fsdp"), None, None, None)),
        check_vma=False,
    )
```

time: 116 us -> 106 us (0.914); the launches traced: 114 us -> 106 us
  local copies, waits for them, and re-layouts: 5.44 us -> 0 us
  Pallas kernels: 108 us -> 106 us
    unnamed x8 -> x0, local copies, waits for them, and re-layouts: 5.44 us -> none
    pallas_call x1 -> x2, Pallas kernels: 108 us -> 106 us  [the longest x1 104 us: local(): pl.pallas_call(functools.partial(exchange, sizes), out_shape=(pltpu.VMEM(...]
where the time goes in v2:
time: 106 us
  Pallas kernels  106 us (100%)
    pallas_call x1, Pallas kernels, local(): pl.pallas_call(functools.partial(exchange, sizes), out_shape=(pltpu.VMEM(...  104 us

profile of v2, /device:TPU:1, one launch (start us, length us, event | category | flops | bytes accessed | tf_op | source)
XLA Modules:
  0.0 106.2 jit_solution(5160580102648453376)
XLA Ops:
  0.6 104.0 %shard_map.50 = (bf16[4,16,4608]{2,1,0:T(8,128)(2,1)S(1)}, bf16[2,2,512,512]{3,2,1,0:T(8,128)(2,1)S(1)}) custom-call(s32[36]{0:T(128)} %owners_ref.1, bf16[4,16,4608]{2,1,0:T(8,128)(2,1)} %grads_ref.1, bf16[2,2,512,512]{3,2,1,0:T(8,128)(2,1)} %roots_ref.1), custom_call_target="tpu_custom_call" | custom-call | flops 2147483648 | bytes 6291456 | tf_op jit(solution)/shard_map/pallas_call | solution.py:187
  104.7 1.5 %shard_map.51 = (bf16[4,16,4608]{2,1,0:T(8,128)(2,1)}, bf16[2,2,512,512]{3,2,1,0:T(8,128)(2,1)}) custom-call(bf16[4,16,4608]{2,1,0:T(8,128)(2,1)S(1)} %get-tuple-element.4.dir_in, bf16[2,2,512,512]{3,2,1,0:T(8,128)(2,1)S(1)} %get-tuple-element.5.grams_in), custom_call_target="tpu_custom_call" | custom-call | tf_op jit(solution)/shard_map/pallas_call | solution.py:216

commit v3 on v2

--- a/solution.py
+++ b/solution.py
@@ -8,6 +8,7 @@
 from jax.sharding import PartitionSpec as P
 
 MESH = pl.DeviceIdType.MESH
+FIRST = 8
 
 
 def rings(chips):
@@ -23,8 +24,8 @@
 
 
 def exchange(
-    sizes, owners_ref, grads_ref, roots_ref, dir_v, grams_v,
-    gv, packed, blocks, roots_v, outgoing, returned, table_v, table, owners,
+    sizes, owners_ref, grads_ref, roots_ref, returned, grams_v, spots,
+    pieces, packed, blocks, roots_v, outgoing, table_v, table, owners,
     load_sem, table_sem, roots_sem, near_sem, send_sem, recv_sem,
 ):
     devices, slabs, ncol, rows, order, slots = sizes
@@ -42,18 +43,17 @@
             semaphore, inc=1, device_id={"fsdp": to}, device_id_type=MESH
         )
 
+    owners_copy = pltpu.make_async_copy(owners_ref, owners, table_sem)
+    owners_copy.start()
     barrier = pltpu.get_barrier_semaphore()
     for step, other in groups[0]:
         signal(barrier, device(step, other))
-
-    owners_copy = pltpu.make_async_copy(owners_ref, owners, table_sem)
-    owners_copy.start()
     loads = []
     for k in range(total):
         s, j = divmod(k, ncol)
         loads.append(
             pltpu.make_async_copy(
-                grads_ref.at[s, :, pl.ds(j * order, order)], gv.at[k], load_sem.at[k]
+                grads_ref.at[s, :, pl.ds(j * order, order)], pieces.at[k], load_sem.at[k]
             )
         )
     for copy in loads:
@@ -79,13 +79,7 @@
     mine = pl.ds(pl.multiple_of(me * rows, rows), rows)
 
     def pack(m, d):
-        packed[m, d] = gv[jnp.maximum(table[m, 0, d], 0)]
-
-    for m in range(slots):
-        pack(m, me)
-        pltpu.make_async_copy(
-            packed.at[m, me], blocks.at[m, mine, :], recv_sem.at[0, m]
-        ).start()
+        packed[m, d] = pieces[jnp.maximum(table[m, 0, d], 0)]
 
     for stage, group in enumerate(groups):
         if stage == 0:
@@ -108,8 +102,16 @@
                     device_id_type=MESH,
                 ).start()
 
+    for m in range(slots):
+        pack(m, me)
+        pltpu.make_async_copy(
+            packed.at[m, me], blocks.at[m, mine, :], recv_sem.at[0, m]
+        ).start()
+    for k in range(total):
+        owner = owners[k]
+        spots[k] = jnp.where(table[0, 0, owner] == k, owner, owner + devices)
+
     roots_copy.wait()
-    backward = [partner for group in groups for partner in group][::-1]
     for m in range(slots):
         pltpu.make_async_copy(blocks.at[m], blocks.at[m], recv_sem.at[0, m]).wait()
         block = blocks[m]
@@ -119,18 +121,37 @@
         outgoing[m] = jnp.dot(
             roots_v[m, 0], product, preferred_element_type=jnp.float32
         ).astype(jnp.bfloat16)
-        for step, other in backward:
-            to = device(step, other)
+
+        def give(to, m=m):
             pltpu.make_async_remote_copy(
                 src_ref=outgoing.at[m, pl.ds(pl.multiple_of(to * rows, rows), rows), :],
-                dst_ref=returned.at[m, me],
+                dst_ref=returned.at[m * devices + me],
                 send_sem=send_sem.at[1, m],
                 recv_sem=recv_sem.at[1, m],
                 device_id={"fsdp": to},
                 device_id_type=MESH,
             ).start()
+
+        early = FIRST if m == slots - 1 else 0
+        for chip in range(early):
+
+            @pl.when(chip != z)
+            def _(chip=chip):
+                give(chip * 2 + core)
+                give(chip * 2 + 1 - core)
+
+        for distance in range(chips // 2, 0, -1):
+            for step in sorted({distance, chips - distance}):
+                chip = lax.rem(z + step, chips)
+
+                @pl.when(chip >= early)
+                def _(chip=chip):
+                    give(chip * 2 + core)
+                    give(chip * 2 + 1 - core)
+
+        give(device(0, 1))
         pltpu.make_async_copy(
-            outgoing.at[m, mine, :], returned.at[m, me], recv_sem.at[1, m]
+            outgoing.at[m, mine, :], returned.at[m * devices + me], recv_sem.at[1, m]
         ).start()
         kept = jnp.where(table[m, 0, me] >= 0, block, jnp.zeros_like(block))
         grams_v[m, 0] = lax.dot_general(
@@ -141,29 +162,37 @@
         ).astype(jnp.bfloat16)
 
     others = pl.ds(0, devices - 1)
-    for m in range(slots):
+    for phase in range(2):
+        for m in range(slots):
+            pltpu.make_async_copy(
+                packed.at[m, others], packed.at[m, others], send_sem.at[phase, m]
+            ).wait()
+            if phase == 1:
+                part = pl.ds(m * devices, devices)
+                pltpu.make_async_copy(
+                    returned.at[part], returned.at[part], recv_sem.at[1, m]
+                ).wait()
+
+
+def store(sizes, spots, returned, grams_in, dir_ref, grams_ref, sems):
+    devices, slabs, ncol, rows, order, slots = sizes
+    total = slabs * ncol
+    copies = [
         pltpu.make_async_copy(
-            packed.at[m, others], packed.at[m, others], send_sem.at[0, m]
-        ).wait()
-    for m in range(slots):
-        pltpu.make_async_copy(
-            packed.at[m, others], packed.at[m, others], send_sem.at[1, m]
-        ).wait()
-        pltpu.make_async_copy(
-            returned.at[m], returned.at[m], recv_sem.at[1, m]
-        ).wait()
+            grams_in.at[m, i], grams_ref.at[m, i], sems.at[total + 2 * m + i]
+        )
+        for m in range(slots)
+        for i in range(2)
+    ]
     for k in range(total):
         s, j = divmod(k, ncol)
-        owner = owners[k]
-        slot = jnp.where(table[0, 0, owner] == k, 0, 1)
-        dir_v[s, :, j * order : (j + 1) * order] = returned[slot, owner]
-
-
-def store(dir_in, grams_in, dir_ref, grams_ref, sems):
-    copies = [
-        pltpu.make_async_copy(grams_in, grams_ref, sems.at[0]),
-        pltpu.make_async_copy(dir_in, dir_ref, sems.at[1]),
-    ]
+        copies.append(
+            pltpu.make_async_copy(
+                returned.at[spots[k]],
+                dir_ref.at[s, :, pl.ds(j * order, order)],
+                sems.at[k],
+            )
+        )
     for copy in copies:
         copy.start()
     for copy in copies:
@@ -179,23 +208,27 @@
     sizes = (devices, slabs, ncol, rows, order, slots)
     hbm = pl.BlockSpec(memory_space=pltpu.HBM)
     vmem = pl.BlockSpec(memory_space=pltpu.VMEM)
+    smem = pl.BlockSpec(memory_space=pltpu.SMEM)
     bf16 = jnp.bfloat16
     stages = len(rings(devices // 2))
     owners, grads, roots = (
         pltpu.with_memory_space_constraint(x, pltpu.HBM) for x in (owners, grads, roots)
     )
-    direction, grams = pl.pallas_call(
+    returned, grams, spots = pl.pallas_call(
         functools.partial(exchange, sizes),
-        out_shape=(pltpu.VMEM(grads.shape, bf16), pltpu.VMEM(roots.shape, bf16)),
+        out_shape=(
+            pltpu.VMEM((slots * devices, rows, order), bf16),
+            pltpu.VMEM(roots.shape, bf16),
+            pltpu.SMEM((total,), jnp.int32),
+        ),
         in_specs=[hbm, hbm, hbm],
-        out_specs=(vmem, vmem),
+        out_specs=(vmem, vmem, smem),
         scratch_shapes=[
             pltpu.VMEM((total, rows, order), bf16),
             pltpu.VMEM((slots, devices, rows, order), bf16),
             pltpu.VMEM((slots, order, order), bf16),
             pltpu.VMEM(roots.shape, bf16),
             pltpu.VMEM((slots, order, order), bf16),
-            pltpu.VMEM((slots, devices, rows, order), bf16),
             pltpu.VMEM((2, 8, 128), jnp.int32),
             pltpu.SMEM((2, 8, 128), jnp.int32),
             pltpu.SMEM((total,), jnp.int32),
@@ -214,16 +247,16 @@
         ),
     )(owners, grads, roots)
     return pl.pallas_call(
-        store,
+        functools.partial(store, sizes),
         out_shape=(
             jax.ShapeDtypeStruct(grads.shape, bf16),
             jax.ShapeDtypeStruct(roots.shape, bf16),
         ),
-        in_specs=[vmem, vmem],
+        in_specs=[smem, vmem, vmem],
         out_specs=(hbm, hbm),
-        scratch_shapes=[pltpu.SemaphoreType.DMA((2,))],
+        scratch_shapes=[pltpu.SemaphoreType.DMA((total + 2 * slots,))],
         compiler_params=pltpu.CompilerParams(vmem_limit_bytes=16 << 20),
-    )(direction, grams)
+    )(spots, returned, grams)
 
 
 def solution(mesh):

time: 106 us -> 103 us (0.972); the launches traced: 106 us -> 101 us
  Pallas kernels: 106 us -> 101 us
    pallas_call x1, Pallas kernels: 104 us -> 98.7 us  [local(): pl.pallas_call(functools.partial(exchange, sizes), out_shape=(pltpu.VMEM(...]
where the time goes in v3:
time: 103 us; the launch traced here: 101 us
  Pallas kernels  101 us (98%)
    pallas_call x1, Pallas kernels, local(): pl.pallas_call(functools.partial(exchange, sizes), out_shape=(pltpu.VMEM(...  98.7 us

profile of v3, /device:TPU:1, one launch (start us, length us, event | category | flops | bytes accessed | tf_op | source)
XLA Modules:
  0.0 101.2 jit_solution(12290343017054084696)
XLA Ops:
  0.6 98.7 %shard_map.50 = (bf16[64,16,512]{2,1,0:T(8,128)(2,1)S(1)}, bf16[2,2,512,512]{3,2,1,0:T(8,128)(2,1)S(1)}, s32[36]{0:T(128)S(4)}) custom-call(s32[36]{0:T(128)} %owners_ref.1, bf16[4,16,4608]{2,1,0:T(8,128)(2,1)} %grads_ref.1, bf16[2,2,512,512]{3,2,1,0:T(8,128)(2,1)} %roots_ref.1), custom_call_target="tpu_custom_call" | custom-call | flops 2147483648 | bytes 6291456 | tf_op jit(solution)/shard_map/pallas_call | solution.py:217
  99.3 1.8 %shard_map.51 = (bf16[4,16,4608]{2,1,0:T(8,128)(2,1)}, bf16[2,2,512,512]{3,2,1,0:T(8,128)(2,1)}) custom-call(s32[36]{0:T(128)S(4)} %get-tuple-element.5.spots, bf16[64,16,512]{2,1,0:T(8,128)(2,1)S(1)} %get-tuple-element.6.returned, bf16[2,2,512,512]{3,2,1,0:T(8,128)(2,1)S(1)} %get-tuple-element.7.grams_in), custom_call_target="tpu_custom_call" | custom-call | tf_op jit(solution)/shard_map/pallas_call | solution.py:249

commit v4 on v3

--- a/solution.py
+++ b/solution.py
@@ -174,27 +174,22 @@
                 ).wait()
 
 
-def store(sizes, spots, returned, grams_in, dir_ref, grams_ref, sems):
+def store(sizes, spots, returned, grams_in, dir_ref, grams_ref, dir_v, sems):
     devices, slabs, ncol, rows, order, slots = sizes
-    total = slabs * ncol
     copies = [
-        pltpu.make_async_copy(
-            grams_in.at[m, i], grams_ref.at[m, i], sems.at[total + 2 * m + i]
-        )
+        pltpu.make_async_copy(grams_in.at[m, i], grams_ref.at[m, i], sems.at[2 * m + i])
         for m in range(slots)
         for i in range(2)
     ]
-    for k in range(total):
-        s, j = divmod(k, ncol)
-        copies.append(
-            pltpu.make_async_copy(
-                returned.at[spots[k]],
-                dir_ref.at[s, :, pl.ds(j * order, order)],
-                sems.at[k],
-            )
-        )
     for copy in copies:
         copy.start()
+    for s in range(slabs):
+        for j in range(ncol):
+            dir_v[s, :, j * order : (j + 1) * order] = returned[spots[s * ncol + j]]
+        copies.append(
+            pltpu.make_async_copy(dir_v.at[s], dir_ref.at[s], sems.at[2 * slots + s])
+        )
+        copies[-1].start()
     for copy in copies:
         copy.wait()
 
@@ -254,7 +249,10 @@
         ),
         in_specs=[smem, vmem, vmem],
         out_specs=(hbm, hbm),
-        scratch_shapes=[pltpu.SemaphoreType.DMA((total + 2 * slots,))],
+        scratch_shapes=[
+            pltpu.VMEM(grads.shape, bf16),
+            pltpu.SemaphoreType.DMA((2 * slots + slabs,)),
+        ],
         compiler_params=pltpu.CompilerParams(vmem_limit_bytes=16 << 20),
     )(spots, returned, grams)
 

time: 103 us -> 103 us (level)
  no operation moved by 1% of the time
where the time goes in v4:
time: 103 us; the launch traced here: 101 us
  Pallas kernels  100 us (97%)
    pallas_call x1, Pallas kernels, local(): pl.pallas_call(functools.partial(exchange, sizes), out_shape=(pltpu.VMEM(...  98.7 us

profile of v4, /device:TPU:1, one launch (start us, length us, event | category | flops | bytes accessed | tf_op | source)
XLA Modules:
  0.0 100.9 jit_solution(1339407513080999093)
XLA Ops:
  0.6 98.7 %shard_map.50 = (bf16[64,16,512]{2,1,0:T(8,128)(2,1)S(1)}, bf16[2,2,512,512]{3,2,1,0:T(8,128)(2,1)S(1)}, s32[36]{0:T(128)S(4)}) custom-call(s32[36]{0:T(128)} %owners_ref.1, bf16[4,16,4608]{2,1,0:T(8,128)(2,1)} %grads_ref.1, bf16[2,2,512,512]{3,2,1,0:T(8,128)(2,1)} %roots_ref.1), custom_call_target="tpu_custom_call" | custom-call | flops 2147483648 | bytes 6291456 | tf_op jit(solution)/shard_map/pallas_call | solution.py:212
  99.3 1.6 %shard_map.51 = (bf16[4,16,4608]{2,1,0:T(8,128)(2,1)}, bf16[2,2,512,512]{3,2,1,0:T(8,128)(2,1)}) custom-call(s32[36]{0:T(128)S(4)} %get-tuple-element.5.spots, bf16[64,16,512]{2,1,0:T(8,128)(2,1)S(1)} %get-tuple-element.6.returned, bf16[2,2,512,512]{3,2,1,0:T(8,128)(2,1)S(1)} %get-tuple-element.7.grams_in), custom_call_target="tpu_custom_call" | custom-call | tf_op jit(solution)/shard_map/pallas_call | solution.py:244
